TPU v7x, 512 devices: a whole 4x8x8 slice. The times are simulated.
512 devices in a mesh: wide: 64 (over y, x, z_lo), narrow: 8 (over z_hi, core).
Axes of the slice: x: 4, y: 8, z: 8 (z_hi: 4, z_lo: 2; z = z_hi * 2 + z_lo), core: 2. Of those that a mesh axis runs over, the one named last changes fastest.
Arguments:
- tval: bfloat16 [4096, 12, 128, 128], P(('wide', 'narrow')), may hold values from -0.16992188 to 0.16992188
- tcol: int32 [4096, 12], replicated, may hold values from 0 to 4095, as said below
- ocol: int32 [4096, 12], P(('wide', 'narrow')), may hold values from 0 to 4095, as said below
- basis: bfloat16 [524288, 128], P(('wide', 'narrow')), may hold values from -6 to 6
Outputs:
- projected: bfloat16 [524288, 128], P(('wide', 'narrow'))
- level: float32 [128, 128], replicated
Inputs may be any that keep to these rules, and one draw needn't show every extreme that they name: `tcol`: the 12 block columns of row i are distinct, include i, and each lies within cyclic distance 8 of i modulo 4096. `ocol`: the 12 block columns of row i are distinct, include i, and each lies within cyclic distance 8 of i modulo 4096.
All inputs are finite; a program needn't handle non-finite values.
Results may differ from a plain program's by a relative error of at most 0.0049.
Values may be sent and summed in bfloat16 or wider, within the bound.
No kernel may reach another device: no remote copies, remote signals or barrier semaphores. Data moves between devices by JAX's collectives and lax.ppermute only.
A program may use at most 64 MiB of HBM per device.

v0:
```python
import jax
import jax.numpy as jnp
from jax import lax
from jax.sharding import PartitionSpec as P


def with_halo(cells, sides, width):
    for axis, dim in sides:
        count = lax.axis_size(axis)
        head = lax.slice_in_dim(cells, 0, width, axis=dim)
        tail = lax.slice_in_dim(cells, cells.shape[dim] - width, cells.shape[dim], axis=dim)
        cells = jnp.concatenate(
            [
                lax.ppermute(tail, axis, [(i, (i + 1) % count) for i in range(count)]),
                cells,
                lax.ppermute(head, axis, [((i + 1) % count, i) for i in range(count)]),
            ],
            axis=dim,
        )
    return cells


def per_device(tval, tcol, ocol, basis):
    local = tval.shape[0]
    size = tval.shape[2]
    width = basis.shape[1]
    slots = tval.shape[1]
    devices = lax.axis_size(("wide", "narrow"))
    count = local * devices
    first = lax.axis_index(("wide", "narrow")) * local
    extended = with_halo(tval, ((("wide", "narrow"), 0),), local)
    basis_ext = with_halo(basis, ((("wide", "narrow"), 0),), local * size)
    basis_blocks = basis_ext.reshape(3 * local, size, width)
    slot_ids = jnp.arange(slots, dtype=jnp.int32)

    def one_row(index):
        glob = first + index
        cols = tcol[glob]
        places = (cols - first + local) % count
        pattern = tcol[cols]
        outcols = ocol[index]
        match = (pattern[None, :, :] == outcols[:, None, None]).astype(jnp.int32)
        which = jnp.sum(match * slot_ids[None, None, :], axis=2)
        valid = jnp.sum(match, axis=2).astype(jnp.bfloat16)
        chosen = extended[places[None, :], which]
        selected = chosen * valid[:, :, None, None]
        square = jnp.einsum(
            "sab,osbc->oac", tval[index], selected, preferred_element_type=jnp.float32
        ).astype(jnp.bfloat16)
        picked = basis_blocks[(outcols - first + local) % count]
        result = jnp.einsum("oac,ock->ak", square, picked, preferred_element_type=jnp.float32)
        return result.astype(jnp.bfloat16)

    projected = lax.map(one_row, jnp.arange(local, dtype=jnp.int32)).reshape(local * size, width)
    partial_level = jnp.dot(basis.T, projected, preferred_element_type=jnp.float32)
    level = lax.psum(partial_level, ("wide", "narrow"))
    level = level / jnp.sqrt(jnp.float32(count * size))
    return (projected, level)


def solution(mesh):
    return jax.shard_map(
        per_device,
        mesh=mesh,
        in_specs=(
            P(("wide", "narrow"), None, None, None),
            P(),
            P(("wide", "narrow"), None),
            P(("wide", "narrow"), None),
        ),
        out_specs=(P(("wide", "narrow"), None), P()),
        check_vma=False,
    )
```

profile of v0, /device:TPU:1, one launch (start us, length us, event | category | flops | bytes accessed | tf_op | source)
XLA Modules:
  0.0 650.9 jit_solution(2711179265260050932)
XLA Ops:
  7.2 7.2 %collective-permute-start = (bf16[8,12,128,128]{3,2,1,0:T(8,128)(2,1)}, bf16[8,12,128,128]{3,2,1,0:T(8,128)(2,1)}, u32[]{:S(2)}, u32[]{:S(2)}) collective-permute-start(bf16[8,12,128,128]{3,2,1,0:T(8,128)(2,1)} %param.6), channel_id=1, source_target_pairs={{0,1},{1,2},{2,3},{3,4},{4,5},{5,6},{6,7},{7,8},{8,9},{9,10},{10,1... | collective-permute-start | bytes 9437192 | tf_op jit(solution)/shard_map/ppermute | solution.py:14
  14.4 3.5 collective-permute-start.1
  20.9 9.1 %collective-permute-start.3 = (bf16[1024,128]{1,0:T(8,128)(2,1)}, bf16[1024,128]{1,0:T(8,128)(2,1)S(1)}, u32[]{:S(2)}, u32[]{:S(2)}) collective-permute-start(bf16[1024,128]{1,0:T(8,128)(2,1)} %param.9), channel_id=1, source_target_pairs={{1,0},{2,1},{3,2},{4,3},{5,4},{6,5},{7,6},{8,7},{9,8},{10,9},{11,1... | collective-permute-start | bytes 786440 | tf_op jit(solution)/shard_map/ppermute | solution.py:16
  31.6 55.9 %collective-permute-done.2 = bf16[1024,128]{1,0:T(8,128)(2,1)S(1)} collective-permute-done((bf16[1024,128]{1,0:T(8,128)(2,1)}, bf16[1024,128]{1,0:T(8,128)(2,1)S(1)}, u32[]{:S(2)}, u32[]{:S(2)}) %collective-permute-start.2) | collective-permute-done | bytes 262176 | tf_op jit(solution)/shard_map/ppermute | solution.py:14
  87.5 6.0 collective-permute-done.3
  94.5 7.7 %pad_maximum_fusion = bf16[24,12,128,128]{3,2,1,0:T(8,128)(2,1)} fusion(bf16[8,12,128,128]{3,2,1,0:T(8,128)(2,1)} %collective-permute-done.1, bf16[8,12,128,128]{3,2,1,0:T(8,128)(2,1)} %param.6, bf16[8,12,128,128]{3,2,1,0:T(8,128)(2,1)} %collective-permute-done), kind=kLoop, calls=%fused_computation.47 | loop fusion | flops 9437184 | bytes 18874368 | tf_op jit(solution)/shard_map/concatenate | solution.py:12
  102.2 269.6 %while.13 = (s32[]{:T(128)}, bf16[8,128,128]{2,1,0:T(8,128)(2,1)}, s32[8]{0:T(128)S(1)}, s32[]{:T(128)}, s32[4096,12]{1,0:T(8,128)S(1)}, /*index=5*/s32[8,12]{1,...) while((s32[]{:T(128)}, bf16[8,128,128]{2,1,0:T(8,128)(2,1)}, ...), condition=%wide.region_3.4_spmd.clone, body=%wide.region_0.3_spmd.clone.sunk | while | flops 656895552 | bytes 25215700 | solution.py:54
  108.0 15.8 %gather_fusion.2 = bf16[144,128,128]{2,1,0:T(8,128)(2,1)} fusion(bf16[24,12,128,128]{3,2,1,0:T(8,128)(2,1)} %get-tuple-element.305, s32[144]{0:T(256)S(1)} %reshape.191), kind=kCustom, calls=%fused_computation.1.clone.clone.1 | custom fusion | bytes 9438336 | tf_op jit(solution)/shard_map/while/body/eval_jaxpr/gather | solution.py:45
  123.8 6.7 %copy.17 = bf16[12,12,128,128]{2,3,1,0:T(8,128)(2,1)} copy(bf16[12,12,128,128]{3,2,1,0:T(8,128)(2,1)} %bitcast.95) | data formatting | bytes 9437184 | tf_op jit(solution)/shard_map/while/body/eval_jaxpr/gather | solution.py:45
  131.1 4.8 fusion.66
  141.7 15.8 %gather_fusion.2 = bf16[144,128,128]{2,1,0:T(8,128)(2,1)} fusion(bf16[24,12,128,128]{3,2,1,0:T(8,128)(2,1)} %get-tuple-element.305, s32[144]{0:T(256)S(1)} %reshape.191), kind=kCustom, calls=%fused_computation.1.clone.clone.1 | custom fusion | bytes 9438336 | tf_op jit(solution)/shard_map/while/body/eval_jaxpr/gather | solution.py:45
  157.5 6.7 %copy.17 = bf16[12,12,128,128]{2,3,1,0:T(8,128)(2,1)} copy(bf16[12,12,128,128]{3,2,1,0:T(8,128)(2,1)} %bitcast.95) | data formatting | bytes 9437184 | tf_op jit(solution)/shard_map/while/body/eval_jaxpr/gather | solution.py:45
  164.8 4.8 fusion.66
  175.4 15.8 %gather_fusion.2 = bf16[144,128,128]{2,1,0:T(8,128)(2,1)} fusion(bf16[24,12,128,128]{3,2,1,0:T(8,128)(2,1)} %get-tuple-element.305, s32[144]{0:T(256)S(1)} %reshape.191), kind=kCustom, calls=%fused_computation.1.clone.clone.1 | custom fusion | bytes 9438336 | tf_op jit(solution)/shard_map/while/body/eval_jaxpr/gather | solution.py:45
  191.2 6.7 %copy.17 = bf16[12,12,128,128]{2,3,1,0:T(8,128)(2,1)} copy(bf16[12,12,128,128]{3,2,1,0:T(8,128)(2,1)} %bitcast.95) | data formatting | bytes 9437184 | tf_op jit(solution)/shard_map/while/body/eval_jaxpr/gather | solution.py:45
  198.5 4.8 fusion.66
  209.1 15.8 %gather_fusion.2 = bf16[144,128,128]{2,1,0:T(8,128)(2,1)} fusion(bf16[24,12,128,128]{3,2,1,0:T(8,128)(2,1)} %get-tuple-element.305, s32[144]{0:T(256)S(1)} %reshape.191), kind=kCustom, calls=%fused_computation.1.clone.clone.1 | custom fusion | bytes 9438336 | tf_op jit(solution)/shard_map/while/body/eval_jaxpr/gather | solution.py:45
  224.9 6.7 %copy.17 = bf16[12,12,128,128]{2,3,1,0:T(8,128)(2,1)} copy(bf16[12,12,128,128]{3,2,1,0:T(8,128)(2,1)} %bitcast.95) | data formatting | bytes 9437184 | tf_op jit(solution)/shard_map/while/body/eval_jaxpr/gather | solution.py:45
  232.2 4.8 fusion.66
  242.8 15.8 %gather_fusion.2 = bf16[144,128,128]{2,1,0:T(8,128)(2,1)} fusion(bf16[24,12,128,128]{3,2,1,0:T(8,128)(2,1)} %get-tuple-element.305, s32[144]{0:T(256)S(1)} %reshape.191), kind=kCustom, calls=%fused_computation.1.clone.clone.1 | custom fusion | bytes 9438336 | tf_op jit(solution)/shard_map/while/body/eval_jaxpr/gather | solution.py:45
  258.6 6.7 %copy.17 = bf16[12,12,128,128]{2,3,1,0:T(8,128)(2,1)} copy(bf16[12,12,128,128]{3,2,1,0:T(8,128)(2,1)} %bitcast.95) | data formatting | bytes 9437184 | tf_op jit(solution)/shard_map/while/body/eval_jaxpr/gather | solution.py:45
  265.9 4.8 fusion.66
  276.5 15.8 %gather_fusion.2 = bf16[144,128,128]{2,1,0:T(8,128)(2,1)} fusion(bf16[24,12,128,128]{3,2,1,0:T(8,128)(2,1)} %get-tuple-element.305, s32[144]{0:T(256)S(1)} %reshape.191), kind=kCustom, calls=%fused_computation.1.clone.clone.1 | custom fusion | bytes 9438336 | tf_op jit(solution)/shard_map/while/body/eval_jaxpr/gather | solution.py:45
  292.3 6.7 %copy.17 = bf16[12,12,128,128]{2,3,1,0:T(8,128)(2,1)} copy(bf16[12,12,128,128]{3,2,1,0:T(8,128)(2,1)} %bitcast.95) | data formatting | bytes 9437184 | tf_op jit(solution)/shard_map/while/body/eval_jaxpr/gather | solution.py:45
  299.7 4.8 fusion.66
  310.2 15.8 %gather_fusion.2 = bf16[144,128,128]{2,1,0:T(8,128)(2,1)} fusion(bf16[24,12,128,128]{3,2,1,0:T(8,128)(2,1)} %get-tuple-element.305, s32[144]{0:T(256)S(1)} %reshape.191), kind=kCustom, calls=%fused_computation.1.clone.clone.1 | custom fusion | bytes 9438336 | tf_op jit(solution)/shard_map/while/body/eval_jaxpr/gather | solution.py:45
  326.1 6.7 %copy.17 = bf16[12,12,128,128]{2,3,1,0:T(8,128)(2,1)} copy(bf16[12,12,128,128]{3,2,1,0:T(8,128)(2,1)} %bitcast.95) | data formatting | bytes 9437184 | tf_op jit(solution)/shard_map/while/body/eval_jaxpr/gather | solution.py:45
  333.4 4.8 fusion.66
  343.9 15.8 %gather_fusion.2 = bf16[144,128,128]{2,1,0:T(8,128)(2,1)} fusion(bf16[24,12,128,128]{3,2,1,0:T(8,128)(2,1)} %get-tuple-element.305, s32[144]{0:T(256)S(1)} %reshape.191), kind=kCustom, calls=%fused_computation.1.clone.clone.1 | custom fusion | bytes 9438336 | tf_op jit(solution)/shard_map/while/body/eval_jaxpr/gather | solution.py:45
  359.8 6.7 %copy.17 = bf16[12,12,128,128]{2,3,1,0:T(8,128)(2,1)} copy(bf16[12,12,128,128]{3,2,1,0:T(8,128)(2,1)} %bitcast.95) | data formatting | bytes 9437184 | tf_op jit(solution)/shard_map/while/body/eval_jaxpr/gather | solution.py:45
  367.1 4.8 fusion.66
  373.7 268.7 %all-reduce.2.cloned.1.call-done = f32[128,128]{0,1:T(8,128)} async-done(((f32[128,128]{0,1:T(8,128)}), f32[128,128]{0,1:T(8,128)}) %all-reduce.2.cloned.1.call-update) | async-done | bytes 65552 | tf_op jit(solution)/shard_map/psum | solution.py:56
  (102 shorter events, 40.1 us)
Async XLA Ops:
  7.2 635.3 %all-reduce.2.cloned.1.call-start = ((), (), s32[]{:S(2)}) async-start(), calls=%async_computation | async-start | bytes 131072 | tf_op jit(solution)/shard_map/psum | solution.py:56
  7.2 87.3 %collective-permute-start = (bf16[8,12,128,128]{3,2,1,0:T(8,128)(2,1)}, bf16[8,12,128,128]{3,2,1,0:T(8,128)(2,1)}, u32[]{:S(2)}, u32[]{:S(2)}) collective-permute-start(bf16[8,12,128,128]{3,2,1,0:T(8,128)(2,1)} %param.6), channel_id=1, source_target_pairs={{0,1},{1,2},{2,3},{3,4},{4,5},{5,6},{6,7},{7,8},{8,9},{9,10},{10,1... | collective-permute-start | bytes 9437192 | tf_op jit(solution)/shard_map/ppermute | solution.py:14
  14.4 80.1 %collective-permute-start.1 = (bf16[8,12,128,128]{3,2,1,0:T(8,128)(2,1)}, bf16[8,12,128,128]{3,2,1,0:T(8,128)(2,1)}, u32[]{:S(2)}, u32[]{:S(2)}) collective-permute-start(bf16[8,12,128,128]{3,2,1,0:T(8,128)(2,1)} %param.6), channel_id=1, source_target_pairs={{1,0},{2,1},{3,2},{4,3},{5,4},{6,5},{7,6},{8,7},{9,8},{10,9},{11,1... | collective-permute-start | bytes 9437192 | tf_op jit(solution)/shard_map/ppermute | solution.py:16
  17.9 69.6 %collective-permute-start.2 = (bf16[1024,128]{1,0:T(8,128)(2,1)}, bf16[1024,128]{1,0:T(8,128)(2,1)S(1)}, u32[]{:S(2)}, u32[]{:S(2)}) collective-permute-start(bf16[1024,128]{1,0:T(8,128)(2,1)} %param.9), channel_id=1, source_target_pairs={{0,1},{1,2},{2,3},{3,4},{4,5},{5,6},{6,7},{7,8},{8,9},{9,10},{10,1... | collective-permute-start | bytes 786440 | tf_op jit(solution)/shard_map/ppermute | solution.py:14
  20.9 72.6 %collective-permute-start.3 = (bf16[1024,128]{1,0:T(8,128)(2,1)}, bf16[1024,128]{1,0:T(8,128)(2,1)S(1)}, u32[]{:S(2)}, u32[]{:S(2)}) collective-permute-start(bf16[1024,128]{1,0:T(8,128)(2,1)} %param.9), channel_id=1, source_target_pairs={{1,0},{2,1},{3,2},{4,3},{5,4},{6,5},{7,6},{8,7},{9,8},{10,9},{11,1... | collective-permute-start | bytes 786440 | tf_op jit(solution)/shard_map/ppermute | solution.py:16
  102.2 269.6 %copy-start = (bf16[1024,128]{1,0:T(8,128)(2,1)S(1)}, bf16[1024,128]{1,0:T(8,128)(2,1)}, u32[]{:S(2)}) copy-start(bf16[1024,128]{1,0:T(8,128)(2,1)} %param.9) | copy-start | bytes 786436
Sparse Core Ops, SparseCore 0:
  373.8 268.5 all-reduce.1
where the time goes:
time: 653 us; the launch traced here: 651 us
  waiting for transfers between devices  331 us (51%)
  local copies, waits for them, and re-layouts  197 us (30%)
  matrix products  40 us (6%)
  other arithmetic  25.5 us (4%)
  starting transfers between devices  22.8 us (3%)
  loops' own time  20.3 us (3%)
  between operations  14.1 us (2%)
    psum x1, waiting for transfers between devices, per_device(): level = lax.psum(partial_level, ('wide', 'narrow'))  269 us
    gather x16, local copies, waits for them, and re-layouts, one_row(): chosen = extended[places[None, :], which]  180 us
    ppermute x2, waiting for transfers between devices, with_halo(): lax.ppermute(tail, axis, [(i, (i + 1) % count) for i in range(count)])  55.9 us
    dot_general x8, matrix products, one_row(): jnp.einsum('oac,ock->ak', square, picked, preferred_element_type=jnp.floa...  38.2 us
    another operation x1, loops' own time, per_device(): lax.map(one_row, jnp.arange(local, dtype=jnp.int32))  20.3 us
  transfers between devices with their start and end apart: 5, of which 3 were waited for; matrix products, arithmetic and copies ran while one was open for 0% of the time, Pallas kernels for 0%

commit v1 on v0

--- a/solution.py
+++ b/solution.py
@@ -2,6 +2,11 @@
 import jax.numpy as jnp
 from jax import lax
 from jax.sharding import PartitionSpec as P
+
+
+def axis_by_axis(array, one, other):
+    partial = lax.psum(array, one)
+    return lax.psum(partial, other)
 
 
 def with_halo(cells, sides, width):
@@ -53,7 +58,7 @@
 
     projected = lax.map(one_row, jnp.arange(local, dtype=jnp.int32)).reshape(local * size, width)
     partial_level = jnp.dot(basis.T, projected, preferred_element_type=jnp.float32)
-    level = lax.psum(partial_level, ("wide", "narrow"))
+    level = axis_by_axis(partial_level, "narrow", "wide")
     level = level / jnp.sqrt(jnp.float32(count * size))
     return (projected, level)
 

time: 653 us -> 1000 us (1.53)
  the two profiles are of different devices: /device:TPU:1 before, /device:TPU:70 now
where the time goes in v1:
time: 1000 us
  waiting for transfers between devices  685 us (68%)
  local copies, waits for them, and re-layouts  197 us (20%)
  matrix products  40 us (4%)
  other arithmetic  25.5 us (3%)
  loops' own time  20.3 us (2%)
  starting transfers between devices  20 us (2%)
  between operations  14.1 us (1%)
    psum x1, waiting for transfers between devices, axis_by_axis(): return lax.psum(partial, other)  536 us
    gather x16, local copies, waits for them, and re-layouts, one_row(): chosen = extended[places[None, :], which]  180 us
    psum x1, waiting for transfers between devices, axis_by_axis(): partial = lax.psum(array, one)  75.6 us
    ppermute x2, waiting for transfers between devices, with_halo(): lax.ppermute(tail, axis, [(i, (i + 1) % count) for i in range(count)])  73.8 us
    dot_general x8, matrix products, one_row(): jnp.einsum('oac,ock->ak', square, picked, preferred_element_type=jnp.floa...  38.2 us
    another operation x1, loops' own time, per_device(): lax.map(one_row, jnp.arange(local, dtype=jnp.int32))  20.3 us
  transfers between devices with their start and end apart: 6, of which 3 were waited for; matrix products, arithmetic and copies ran while one was open for 0% of the time, Pallas kernels for 0%

profile of v1, /device:TPU:70, one launch (start us, length us, event | category | flops | bytes accessed | tf_op | source)
XLA Modules:
  0.0 1002.5 jit_solution(6534565014307304934)
XLA Ops:
  7.2 1.9 collective-permute-start
  9.1 9.5 collective-permute-start.1
  20.5 6.7 collective-permute-start.3
  28.8 73.8 %collective-permute-done.2 = bf16[1024,128]{1,0:T(8,128)(2,1)S(1)} collective-permute-done((bf16[1024,128]{1,0:T(8,128)(2,1)}, bf16[1024,128]{1,0:T(8,128)(2,1)S(1)}, u32[]{:S(2)}, u32[]{:S(2)}) %collective-permute-start.2) | collective-permute-done | bytes 262176 | tf_op jit(solution)/shard_map/ppermute | solution.py:19
  103.7 7.7 pad_maximum_fusion
  111.4 269.6 %while.13 = (s32[]{:T(128)}, bf16[8,128,128]{2,1,0:T(8,128)(2,1)}, s32[8]{0:T(128)S(1)}, s32[]{:T(128)}, s32[4096,12]{1,0:T(8,128)S(1)}, /*index=5*/s32[8,12]{1,...) while((s32[]{:T(128)}, bf16[8,128,128]{2,1,0:T(8,128)(2,1)}, ...), condition=%wide.region_3.4_spmd.clone, body=%wide.region_0.3_spmd.clone.sunk | while | flops 656895552 | bytes 25215700 | solution.py:59
  117.1 15.8 %gather_fusion.2 = bf16[144,128,128]{2,1,0:T(8,128)(2,1)} fusion(bf16[24,12,128,128]{3,2,1,0:T(8,128)(2,1)} %get-tuple-element.305, s32[144]{0:T(256)S(1)} %reshape.191), kind=kCustom, calls=%fused_computation.1.clone.clone.1 | custom fusion | bytes 9438336 | tf_op jit(solution)/shard_map/while/body/eval_jaxpr/gather | solution.py:50
  132.9 6.7 copy.17
  140.3 4.8 fusion.66
  150.8 15.8 %gather_fusion.2 = bf16[144,128,128]{2,1,0:T(8,128)(2,1)} fusion(bf16[24,12,128,128]{3,2,1,0:T(8,128)(2,1)} %get-tuple-element.305, s32[144]{0:T(256)S(1)} %reshape.191), kind=kCustom, calls=%fused_computation.1.clone.clone.1 | custom fusion | bytes 9438336 | tf_op jit(solution)/shard_map/while/body/eval_jaxpr/gather | solution.py:50
  166.6 6.7 copy.17
  174.0 4.8 fusion.66
  184.5 15.8 %gather_fusion.2 = bf16[144,128,128]{2,1,0:T(8,128)(2,1)} fusion(bf16[24,12,128,128]{3,2,1,0:T(8,128)(2,1)} %get-tuple-element.305, s32[144]{0:T(256)S(1)} %reshape.191), kind=kCustom, calls=%fused_computation.1.clone.clone.1 | custom fusion | bytes 9438336 | tf_op jit(solution)/shard_map/while/body/eval_jaxpr/gather | solution.py:50
  200.4 6.7 copy.17
  207.7 4.8 fusion.66
  218.2 15.8 %gather_fusion.2 = bf16[144,128,128]{2,1,0:T(8,128)(2,1)} fusion(bf16[24,12,128,128]{3,2,1,0:T(8,128)(2,1)} %get-tuple-element.305, s32[144]{0:T(256)S(1)} %reshape.191), kind=kCustom, calls=%fused_computation.1.clone.clone.1 | custom fusion | bytes 9438336 | tf_op jit(solution)/shard_map/while/body/eval_jaxpr/gather | solution.py:50
  234.1 6.7 copy.17
  241.4 4.8 fusion.66
  251.9 15.8 %gather_fusion.2 = bf16[144,128,128]{2,1,0:T(8,128)(2,1)} fusion(bf16[24,12,128,128]{3,2,1,0:T(8,128)(2,1)} %get-tuple-element.305, s32[144]{0:T(256)S(1)} %reshape.191), kind=kCustom, calls=%fused_computation.1.clone.clone.1 | custom fusion | bytes 9438336 | tf_op jit(solution)/shard_map/while/body/eval_jaxpr/gather | solution.py:50
  267.8 6.7 copy.17
  275.1 4.8 fusion.66
  285.6 15.8 %gather_fusion.2 = bf16[144,128,128]{2,1,0:T(8,128)(2,1)} fusion(bf16[24,12,128,128]{3,2,1,0:T(8,128)(2,1)} %get-tuple-element.305, s32[144]{0:T(256)S(1)} %reshape.191), kind=kCustom, calls=%fused_computation.1.clone.clone.1 | custom fusion | bytes 9438336 | tf_op jit(solution)/shard_map/while/body/eval_jaxpr/gather | solution.py:50
  301.5 6.7 copy.17
  308.8 4.8 fusion.66
  319.3 15.8 %gather_fusion.2 = bf16[144,128,128]{2,1,0:T(8,128)(2,1)} fusion(bf16[24,12,128,128]{3,2,1,0:T(8,128)(2,1)} %get-tuple-element.305, s32[144]{0:T(256)S(1)} %reshape.191), kind=kCustom, calls=%fused_computation.1.clone.clone.1 | custom fusion | bytes 9438336 | tf_op jit(solution)/shard_map/while/body/eval_jaxpr/gather | solution.py:50
  335.2 6.7 copy.17
  342.5 4.8 fusion.66
  353.1 15.8 %gather_fusion.2 = bf16[144,128,128]{2,1,0:T(8,128)(2,1)} fusion(bf16[24,12,128,128]{3,2,1,0:T(8,128)(2,1)} %get-tuple-element.305, s32[144]{0:T(256)S(1)} %reshape.191), kind=kCustom, calls=%fused_computation.1.clone.clone.1 | custom fusion | bytes 9438336 | tf_op jit(solution)/shard_map/while/body/eval_jaxpr/gather | solution.py:50
  368.9 6.7 copy.17
  376.2 4.8 fusion.66
  382.9 75.6 %all-reduce.3.cloned.1.call-done = f32[128,128]{0,1:T(8,128)} async-done(((f32[128,128]{0,1:T(8,128)}), f32[128,128]{0,1:T(8,128)}) %all-reduce.3.cloned.1.call-update) | async-done | bytes 65552 | tf_op jit(solution)/shard_map/psum | solution.py:8
  458.6 535.5 %all-reduce.5.cloned.1.call-done = f32[128,128]{0,1:T(8,128)} async-done(((f32[128,128]{0,1:T(8,128)}), f32[128,128]{0,1:T(8,128)}) %all-reduce.5.cloned.1.call-update) | async-done | bytes 65552 | tf_op jit(solution)/shard_map/psum | solution.py:9
  (105 shorter events, 39.2 us)
Async XLA Ops:
  7.2 451.4 %all-reduce.3.cloned.1.call-start = ((), (), s32[]{:S(2)}) async-start(), calls=%async_computation | async-start | bytes 131072 | tf_op jit(solution)/shard_map/psum | solution.py:8
  7.2 96.4 %collective-permute-start = (bf16[8,12,128,128]{3,2,1,0:T(8,128)(2,1)}, bf16[8,12,128,128]{3,2,1,0:T(8,128)(2,1)}, u32[]{:S(2)}, u32[]{:S(2)}) collective-permute-start(bf16[8,12,128,128]{3,2,1,0:T(8,128)(2,1)} %param.6), channel_id=1, source_target_pairs={{0,1},{1,2},{2,3},{3,4},{4,5},{5,6},{6,7},{7,8},{8,9},{9,10},{10,1... | collective-permute-start | bytes 9437192 | tf_op jit(solution)/shard_map/ppermute | solution.py:19
  9.1 94.5 %collective-permute-start.1 = (bf16[8,12,128,128]{3,2,1,0:T(8,128)(2,1)}, bf16[8,12,128,128]{3,2,1,0:T(8,128)(2,1)}, u32[]{:S(2)}, u32[]{:S(2)}) collective-permute-start(bf16[8,12,128,128]{3,2,1,0:T(8,128)(2,1)} %param.6), channel_id=1, source_target_pairs={{1,0},{2,1},{3,2},{4,3},{5,4},{6,5},{7,6},{8,7},{9,8},{10,9},{11,1... | collective-permute-start | bytes 9437192 | tf_op jit(solution)/shard_map/ppermute | solution.py:21
  18.6 84.0 %collective-permute-start.2 = (bf16[1024,128]{1,0:T(8,128)(2,1)}, bf16[1024,128]{1,0:T(8,128)(2,1)S(1)}, u32[]{:S(2)}, u32[]{:S(2)}) collective-permute-start(bf16[1024,128]{1,0:T(8,128)(2,1)} %param.9), channel_id=1, source_target_pairs={{0,1},{1,2},{2,3},{3,4},{4,5},{5,6},{6,7},{7,8},{8,9},{9,10},{10,1... | collective-permute-start | bytes 786440 | tf_op jit(solution)/shard_map/ppermute | solution.py:19
  20.5 82.1 %collective-permute-start.3 = (bf16[1024,128]{1,0:T(8,128)(2,1)}, bf16[1024,128]{1,0:T(8,128)(2,1)S(1)}, u32[]{:S(2)}, u32[]{:S(2)}) collective-permute-start(bf16[1024,128]{1,0:T(8,128)(2,1)} %param.9), channel_id=1, source_target_pairs={{1,0},{2,1},{3,2},{4,3},{5,4},{6,5},{7,6},{8,7},{9,8},{10,9},{11,1... | collective-permute-start | bytes 786440 | tf_op jit(solution)/shard_map/ppermute | solution.py:21
  111.4 269.6 %copy-start = (bf16[1024,128]{1,0:T(8,128)(2,1)S(1)}, bf16[1024,128]{1,0:T(8,128)(2,1)}, u32[]{:S(2)}) copy-start(bf16[1024,128]{1,0:T(8,128)(2,1)} %param.9) | copy-start | bytes 786436
  382.9 611.2 %all-reduce.5.cloned.1.call-start = ((), (), s32[]{:S(2)}) async-start(), calls=%async_computation.1 | async-start | bytes 131072 | tf_op jit(solution)/shard_map/psum | solution.py:9
Sparse Core Ops, SparseCore 0:
  383.0 75.5 all-reduce.2
  461.7 532.3 all-reduce.4
